TPU v7x, 32 devices: a whole 2x2x4 slice. The times are simulated.
32 devices in a mesh: grid: 4 (over z), space: 4 (over y, x), spec: 2 (over core).
Axes of the slice: x: 2, y: 2, z: 4, core: 2. Of those that a mesh axis runs over, the one named last changes fastest.
Arguments:
- spectrum: float32 [4, 32, 36, 8, 128], P('grid', None, None, ('space', 'spec')), may hold values from 0.05 to 1
- land_sea: int32 [4, 8, 128], P('grid'), may hold values 0 or 1
- west_index: int32 [4, 8], P('grid'), may hold values from 0 to 7, each once within a row
- east_index: int32 [4, 8], P('grid'), may hold values from 0 to 7, each once within a row
- current_u: float32 [4, 64, 8, 128], P('grid', None, ('space', 'spec')), may hold values from -0.3 to 0.3
- current_v: float32 [4, 64, 8, 128], P('grid', None, ('space', 'spec')), may hold values from -0.3 to 0.3
- transfer: bfloat16 [1152, 1152], replicated, may hold values from -0.1875 to 0.1875
- wind_rate: float32 [36], replicated, may hold values from 0.1 to 1
- dissipation: float32 [36], replicated, may hold values from 0.5 to 4
Outputs:
- waves: float32 [4, 32, 36, 8, 128], P('grid', 'space', 'spec')
- stokes: float32 [4, 128, 8, 128], P('grid', None, ('space', 'spec'))
Inputs may be any that keep to these rules, and one draw needn't show every extreme that they name: `land_sea`: 1 marks a sea cell, 0 a land cell. `west_index`: row g lists, for each row of grid g, the row of grid g - 1 whose easternmost cell borders it; each row of the array is a permutation of the 8 rows. `east_index`: row g lists, for each row of grid g, the row of grid g + 1 whose westernmost cell borders it; each row of the array is a permutation of the 8 rows.
All inputs are finite; a program needn't handle non-finite values. No bound on the sum of `land_sea` on one device may be relied on, other than what follows from the above.
Results may differ from a plain program's by a relative error of at most 0.00082.
Values sent between devices are 32-bit elements; how exact they have to be, the bound alone decides.
A program may use at most 64 MiB of HBM per device.

v0:
```python
import functools
import math

import jax
import jax.numpy as jnp
import numpy as np
from jax import lax
from jax.experimental import pallas as pl
from jax.experimental.pallas import tpu as pltpu
from jax.sharding import PartitionSpec as P

sigma_base = 0.2199
gravity = 9.81
growth = 1.1
courant_scale = 3.0
time_step = 0.5
stokes_gain = 2.0
highest = lax.Precision.HIGHEST
vmem = pl.BlockSpec(memory_space=pltpu.VMEM)
smem = pl.BlockSpec(memory_space=pltpu.SMEM)
params = pltpu.CompilerParams(vmem_limit_bytes=40 * 1024 * 1024)


def tables(freq_count, directions, levels):
    freq_steps = np.arange(freq_count).astype(np.float64)
    radian_freq = sigma_base * growth**freq_steps
    wavenum = radian_freq * radian_freq / gravity
    angles = 2.0 * np.pi * np.arange(directions) / directions
    depths = -(np.arange(levels) + 0.5)
    decays = np.exp(2.0 * wavenum[:, None] * depths[None, :])
    current_weight = decays / np.sum(decays, axis=1, keepdims=True)
    drifts = (radian_freq * wavenum)[:, None] * decays
    drifts = drifts / np.sum(drifts, axis=0, keepdims=True)
    return (angles, current_weight.astype(np.float32), drifts)


def source_kernel(ranks, cores, dir_local, freq_local, blocked, *refs):
    spectra_ref, sea_ref, transfer_ref, gain_ref, damping_ref, out_ref, held = refs
    freq_count = cores * freq_local
    chunks = [
        (
            (s * cores + c) * dir_local * freq_local + d * freq_local,
            (s * dir_local + d) * freq_count + c * freq_local,
        )
        for s in range(ranks)
        for d in range(dir_local)
        for c in range(cores)
    ]
    if blocked:
        for there, here in chunks:
            held[here : here + freq_local, :] = spectra_ref[there : there + freq_local, :]
        spectra = held[...]
    else:
        spectra = spectra_ref[...]
    redist = jnp.dot(
        transfer_ref[...], spectra.astype(jnp.bfloat16), preferred_element_type=jnp.float32
    )
    energy = jnp.sum(spectra * spectra, axis=0, keepdims=True) * (1.0 / spectra.shape[0])
    held[...] = (
        sea_ref[...]
        * (spectra * (1.0 + time_step * gain_ref[...]) + time_step * redist)
        / (1.0 + time_step * damping_ref[...] * energy)
    )
    for there, here in chunks:
        out_ref[there : there + freq_local, :] = held[here : here + freq_local, :]


def sources(spectra, sea_points, transfer, gain, damping, split, blocked):
    return pl.pallas_call(
        functools.partial(source_kernel, *split, blocked),
        out_shape=jax.ShapeDtypeStruct(spectra.shape, jnp.float32),
        in_specs=[vmem] * 5,
        out_specs=vmem,
        scratch_shapes=[pltpu.VMEM(spectra.shape, jnp.float32)],
        compiler_params=params,
        name="sources",
    )(spectra, sea_points, transfer, gain, damping)


def sweep_kernel(rows, dirs, freqs, stride, flow_at, flow_stride, blocked, *refs):
    courant_ref, wave_ref, flow_ref, west_ref, east_ref, sea_ref, out_ref = refs
    columns = wave_ref.shape[-1]
    shape = (rows, columns)
    lane = lax.broadcasted_iota(jnp.int32, shape, 1)
    row = lax.broadcasted_iota(jnp.int32, shape, 0)
    sea = sea_ref[...].astype(jnp.float32)
    first, last = lane == 0, lane == columns - 1
    top, bottom = row == 0, row == rows - 1

    def at_freq(f, carry):
        a = flow_ref[pl.ds(flow_at + f, rows, stride=flow_stride), :]
        b = flow_ref[pl.ds(flow_at + freqs + f, rows, stride=flow_stride), :]
        a_west, a_east = jnp.maximum(a, 0.0), jnp.maximum(-a, 0.0)
        b_north, b_south = jnp.maximum(b, 0.0), jnp.maximum(-b, 0.0)
        for d in range(dirs):
            c = d * freqs + f
            cx, cy = courant_ref[0, c], courant_ref[1, c]
            wave = wave_ref[pl.ds(c, rows, stride=stride), :]
            ghost_west = jnp.where(first, pltpu.roll(west_ref[d], columns - f, 1), 0.0)
            ghost_east = jnp.where(last, pltpu.roll(east_ref[d], columns - 1 - f, 1), 0.0)
            west = jnp.where(first, ghost_west, pltpu.roll(wave, 1, 1))
            east = jnp.where(last, ghost_east, pltpu.roll(wave, columns - 1, 1))
            north = jnp.where(top, 0.0, pltpu.roll(wave, 1, 0))
            south = jnp.where(bottom, 0.0, pltpu.roll(wave, rows - 1, 0))
            moved = (
                wave
                - a_west * (wave - west)
                - a_east * (wave - east)
                - b_north * (wave - north)
                - b_south * (wave - south)
            )
            moved = moved + jnp.maximum(cx, 0.0) * ghost_west + jnp.maximum(-cx, 0.0) * ghost_east
            onward = cx >= 0.0
            speed = jnp.full(shape, jnp.abs(cx), jnp.float32)
            scale = 1.0 / (1.0 + speed)
            ratio = speed * scale
            swept = moved * scale
            place = jnp.where(onward, lane, columns - 1 - lane)
            step = 1
            while step < columns:
                turn = jnp.where(onward, step, columns - step)
                swept = swept + jnp.where(place >= step, ratio, 0.0) * pltpu.roll(swept, turn, 1)
                ratio = ratio * ratio
                step *= 2
            onward = cy >= 0.0
            speed = jnp.full(shape, jnp.abs(cy), jnp.float32)
            scale = 1.0 / (1.0 + speed)
            ratio = speed * scale
            swept = swept * scale
            place = jnp.where(onward, row, rows - 1 - row)
            step = 1
            while step < rows:
                down = pltpu.roll(swept, step, 0)
                up = pltpu.roll(swept, rows - step, 0) if 2 * step != rows else down
                shifted = jnp.where(onward, down, up)
                swept = swept + jnp.where(place >= step, ratio, 0.0) * shifted
                ratio = ratio * ratio
                step *= 2
            if blocked:
                out_ref[pl.ds(c, rows, stride=dirs * freqs), :] = sea * swept
            else:
                out_ref[c] = sea * swept
        return carry

    lax.fori_loop(0, freqs, at_freq, 0)


def neighbour(column, distance):
    devices = range(lax.axis_size("grid"))
    route = [(i - distance, i) for i in devices if i - distance in devices]
    return lax.ppermute(column, "grid", route)


def propagate(wave, flow, flow_at, courant, sea, west_order, east_order, dirs, freqs, blocked):
    rows, held, columns = wave.shape
    comps = dirs * freqs
    edges = (wave[:, :comps, -1], wave[:, :comps, 0])

    def placed(raw, order):
        picked = jnp.take(raw, order, axis=0).reshape(rows, dirs, freqs).transpose(1, 0, 2)
        return jnp.pad(picked, ((0, 0), (0, 0), (0, columns - freqs)))

    west = placed(neighbour(edges[0], 1), west_order)
    east = placed(neighbour(edges[1], -1), east_order)
    shape = (rows * comps, columns) if blocked else (comps, rows, columns)
    return pl.pallas_call(
        functools.partial(
            sweep_kernel, rows, dirs, freqs, held, flow_at, flow.shape[1], blocked
        ),
        out_shape=jax.ShapeDtypeStruct(shape, jnp.float32),
        in_specs=[smem] + [vmem] * 5,
        out_specs=vmem,
        compiler_params=params,
        name="propagate",
    )(courant, wave.reshape(-1, columns), flow.reshape(-1, columns), west, east, sea)


def exchange(payload):
    return lax.all_to_all(payload, ("space", "spec"), split_axis=0, concat_axis=0, tiled=True)


def shards(
    spectrum,
    land_sea,
    west_index,
    east_index,
    current_u,
    current_v,
    transfer,
    wind_rate,
    dissipation,
):
    ranks = lax.axis_size("space")
    cores = lax.axis_size("spec")
    directions, freq_count, rows_local, columns = spectrum.shape[1:]
    levels = current_u.shape[1]
    total_rows = land_sea.shape[1]
    dir_local = directions // ranks
    freq_local = freq_count // cores
    components = directions * freq_count
    comps_local = dir_local * freq_local
    points = rows_local * columns
    groups = ranks * cores
    split = (ranks, cores, dir_local, freq_local)
    space_rank = lax.axis_index("space")
    core_rank = lax.axis_index("spec")
    block_rank = space_rank * cores + core_rank
    angles, current_weight, drifts = tables(freq_count, directions, levels)
    speeds = courant_scale * growth ** (-np.arange(freq_count).astype(np.float64))
    courant = np.stack(
        [np.cos(angles)[:, None] * speeds[None, :], np.sin(angles)[:, None] * speeds[None, :]]
    )
    courant = courant.reshape(2, ranks, dir_local, cores, freq_local).transpose(1, 3, 0, 2, 4)
    courant = courant.reshape(groups, 2, comps_local).astype(np.float32)
    courant = lax.dynamic_index_in_dim(jnp.asarray(courant), block_rank, 0, keepdims=False)

    trig = np.stack([np.cos(angles), np.sin(angles)]) * stokes_gain / math.sqrt(directions)
    stokes_table = trig[:, None, :, None] * drifts.T[None, :, None, :]
    stokes_table = stokes_table.reshape(2 * levels, ranks, dir_local, cores, freq_local)
    stokes_table = stokes_table.transpose(0, 1, 3, 2, 4).reshape(2 * levels, components)
    stokes_table = jnp.asarray(stokes_table.astype(np.float32))

    heading = jnp.asarray((0.5 * (1.0 + np.cos(angles))).astype(np.float32))
    gain = (heading[:, None] * wind_rate[None, :]).reshape(components, 1)
    damping = jnp.broadcast_to(dissipation[None, :], (directions, freq_count))
    damping = damping.reshape(components, 1)
    sea_cells = land_sea[0]
    sea_points = lax.dynamic_slice_in_dim(sea_cells, block_rank * rows_local, rows_local, 0)
    sea_points = sea_points.reshape(1, points).astype(jnp.float32)
    currents = jnp.concatenate(
        [current_u[0].reshape(levels, points), current_v[0].reshape(levels, points)], axis=1
    )
    flow = jnp.dot(jnp.asarray(current_weight), currents, precision=highest)
    flow = flow.reshape(cores, freq_local, 2, points).transpose(0, 2, 1, 3)
    flow = jnp.broadcast_to(
        flow.reshape(1, cores, 2 * freq_local, points), (ranks, cores, 2 * freq_local, points)
    ).reshape(groups, 2 * freq_local, points)

    def by_row(arrived):
        held = arrived.shape[1]
        arrived = arrived.reshape(groups, held, rows_local, columns).transpose(0, 2, 1, 3)
        return arrived.reshape(total_rows, held, columns)

    def step(spectra, blocked):
        return sources(spectra, sea_points, transfer, gain, damping, split, blocked)

    def onward(arrived, flow_part, flow_at, blocked):
        return propagate(
            arrived,
            flow_part,
            flow_at,
            courant,
            sea_cells,
            west_index[0],
            east_index[0],
            dir_local,
            freq_local,
            blocked,
        )

    spectra = step(spectrum[0].reshape(components, points), False)
    blocks = spectra.reshape(groups, comps_local, points)
    first = by_row(exchange(jnp.concatenate([blocks, flow], axis=1)))
    wave = onward(first, first, comps_local, True)
    wave = wave.reshape(groups, rows_local, comps_local, columns).transpose(0, 2, 1, 3)
    returned = exchange(wave.reshape(groups, comps_local, points))
    spectra = step(returned.reshape(components, points), True)
    arrived = by_row(exchange(spectra.reshape(groups, comps_local, points)))
    stokes = jnp.dot(stokes_table, spectra, precision=highest)
    waves = onward(arrived, first, comps_local, False)
    return (
        waves.reshape(1, dir_local, freq_local, total_rows, columns),
        stokes.reshape(1, 2 * levels, rows_local, columns),
    )


def solution(mesh):
    placed = (
        P("grid", None, None, ("space", "spec"), None),
        P("grid", None, None),
        P("grid", None),
        P("grid", None),
        P("grid", None, ("space", "spec"), None),
        P("grid", None, ("space", "spec"), None),
        P(),
        P(),
        P(),
    )
    return jax.shard_map(
        shards,
        mesh=mesh,
        in_specs=placed,
        out_specs=(
            P("grid", "space", "spec", None, None),
            P("grid", None, ("space", "spec"), None),
        ),
        check_vma=False,
    )
```

profile of v0, /device:TPU:0, one launch (start us, length us, event | category | flops | bytes accessed | tf_op | source)
XLA Modules:
  0.0 101.1 jit_solution(1709905578691306629)
XLA Ops:
  0.6 0.7 broadcast_multiply_fusion
  1.4 0.2 mul.31.refs_3_
  1.6 0.0 copy-start.4
  1.6 0.7 broadcast_in_dim.24
  2.3 0.2 reshape.143.refs_4_
  2.5 0.0 copy-start.6
  2.5 1.1 %fusion = f32[36,256]{1,0:T(8,128)S(1)} fusion(f32[36,64]{1,0:T(8,128)} %constant.42.clone, f32[64,128]{1,0:T(8,128)} %bitcast.64, f32[64,128]{1,0:T(8,128)} %bitcast.65), kind=kOutput, calls=%fused_computation.5 | convolution fusion | flops 7094272 | bytes 111616 | tf_op jit(solution)/shard_map/dot_general | solution.py:233
  3.6 0.7 convert_bitcast_fusion.refs_1_
  4.3 0.0 copy-start
  4.3 1.7 %copy-done = bf16[1152,1152]{1,0:T(8,128)(2,1)S(1)} copy-done((bf16[1152,1152]{1,0:T(8,128)(2,1)S(1)}, bf16[1152,1152]{1,0:T(8,128)(2,1)}, u32[]{:S(2)}) %copy-start) | copy-done | bytes 2654232
  6.1 1.1 %copy-done.8 = f32[1,32,36,1,128]{4,3,2,1,0:T(1,128)S(1)} copy-done((f32[1,32,36,1,128]{4,3,2,1,0:T(1,128)S(1)}, f32[1,32,36,1,128]{4,3,2,1,0:T(1,128)}, u32[]{:S(2)}) %copy-start.8) | copy-done | bytes 589848
  7.2 1.0 %sources.2 = f32[1152,128]{1,0:T(8,128)S(1)} custom-call(f32[1152,128]{1,0:T(8,128)S(1)} %bitcast.53, f32[1,128]{1,0:T(1,128)S(1)} %convert_bitcast_fusion.refs_1_, bf16[1152,1152]{1,0:T(8,128)(2,1)S(1)} %copy-done, f32[1152,1]{1,0:T(8,128)S(1)} %mul.31.refs_3_, f32[1152,1]{1,0:T(8,128)S(1)} %reshape.143.refs_4_), custom_call_target="tpu_custom_call" | custom-call | tf_op jit(solution)/shard_map/sources/pallas_call | solution.py:69
  8.2 0.0 copy-done.4
  8.2 0.0 copy-done.6
  8.2 0.0 copy-start.11
  8.2 0.0 copy-start.12
  8.2 0.9 pad_maximum_fusion
  9.2 5.2 %all-to-all-start = ((f32[8,180,128]{2,1,0:T(8,128)}), f32[8,180,128]{2,1,0:T(8,128)S(1)}, u32[]{:S(2)}, u32[]{:S(2)}) async-start(f32[8,180,128]{2,1,0:T(8,128)} %pad_maximum_fusion), calls=%async_computation | async-start | bytes 1507328 | tf_op jit(solution)/shard_map/all_to_all | solution.py:179
  14.4 0.0 copy-done.11
  14.4 0.0 copy-done.12
  14.4 0.0 copy-start.9
  14.5 12.1 %all-to-all-done = f32[8,180,128]{2,1,0:T(8,128)S(1)} async-done(((f32[8,180,128]{2,1,0:T(8,128)}), f32[8,180,128]{2,1,0:T(8,128)S(1)}, u32[]{:S(2)}, u32[]{:S(2)}) %all-to-all-start) | async-done | bytes 737312 | tf_op jit(solution)/shard_map/all_to_all | solution.py:179
  26.6 0.2 fusion.5
  26.8 0.3 copy.50
  27.2 3.5 %collective-permute-start = (f32[8,144]{1,0:T(8,128)S(1)}, f32[8,144]{1,0:T(8,128)S(1)}, u32[]{:S(2)}, u32[]{:S(2)}) collective-permute-start(f32[8,144]{1,0:T(8,128)S(1)} %bitcast.68), channel_id=1, source_target_pairs={{0,8},{8,16},{16,24},{1,9},{9,17},{17,25},{2,10},{10,18},{18,26},{... | collective-permute-start | bytes 13832 | tf_op jit(solution)/shard_map/ppermute | solution.py:151
  30.6 0.7 dynamic-slice_bitcast_fusion.refs_0_
  31.3 0.3 copy.51
  31.7 0.0 copy-done.10
  31.7 1.6 %collective-permute-start.1 = (f32[8,144]{1,0:T(8,128)S(1)}, f32[8,144]{1,0:T(8,128)S(1)}, u32[]{:S(2)}, u32[]{:S(2)}) collective-permute-start(f32[8,144]{1,0:T(8,128)S(1)} %bitcast.67), channel_id=1, source_target_pairs={{8,0},{16,8},{24,16},{9,1},{17,9},{25,17},{10,2},{18,10},{26,18},{... | collective-permute-start | bytes 13832 | tf_op jit(solution)/shard_map/ppermute | solution.py:151
  33.2 1.2 %reshape_reshape_transpose_reshape.8.refs_1_.refs_2_ = f32[1440,128]{1,0:T(8,128)S(1)} reshape(f32[8,180,128]{2,1,0:T(8,128)} %copy-done.10) | data formatting | bytes 1474560 | tf_op jit(solution)/shard_map/reshape;reshape;transpose;reshape | solution.py:175
  34.4 0.0 collective-permute-done
  34.4 0.6 gather_fusion
  35.0 0.1 broadcast_select_fusion.3
  35.1 0.1 reshape.91
  35.1 2.3 %collective-permute-done.1 = f32[8,144]{1,0:T(8,128)S(1)} collective-permute-done((f32[8,144]{1,0:T(8,128)S(1)}, f32[8,144]{1,0:T(8,128)S(1)}, u32[]{:S(2)}, u32[]{:S(2)}) %collective-permute-start.1) | collective-permute-done | bytes 4640 | tf_op jit(solution)/shard_map/ppermute | solution.py:151
  37.5 0.6 gather_fusion.1
  38.0 0.1 broadcast_select_fusion.2
  38.1 0.1 reshape.92
  38.2 0.0 copy-done.9
  38.3 11.6 %propagate.2 = f32[1152,128]{1,0:T(8,128)S(1)} custom-call(f32[2,144]{1,0:T(2,128)S(1)} %dynamic-slice_bitcast_fusion.refs_0_, f32[1440,128]{1,0:T(8,128)S(1)} %reshape_reshape_transpose_reshape.8.refs_1_.refs_2_, f32[1440,128]{1,0:T(8,128)S(1)} %reshape_reshape_transpose_reshape.8.refs_1_.refs_2_, f32[8,8,128]{2,1,0:T(8,128)S(1)} %pad.13.refs_3_, ...), custom_call_target="tpu_custom_call" | custom-call | tf_op jit(solution)/shard_map/propagate/pallas_call | solution.py:166
  49.8 12.8 %all_to_all.15 = f32[8,144,128]{2,1,0:T(8,128)S(1)} all-to-all(f32[8,144,128]{2,1,0:T(8,128)S(1)} %bitcast.50), channel_id=1, replica_groups=mesh['grid'=4,'space'=4,'spec'=2] {'space','spec'}, dimensions={0} | all-to-all | bytes 1179648 | tf_op jit(solution)/shard_map/all_to_all | solution.py:179
  62.7 0.0 copy-done.1
  62.7 0.0 copy-done.5
  62.7 0.0 copy-done.7
  62.7 1.1 %sources.3 = f32[1152,128]{1,0:T(8,128)S(1)} custom-call(f32[1152,128]{1,0:T(8,128)S(1)} %bitcast.51, f32[1,128]{1,0:T(1,128)S(1)} %convert_bitcast_fusion.refs_1_, bf16[1152,1152]{1,0:T(8,128)(2,1)S(1)} %copy-done.1, f32[1152,1]{1,0:T(8,128)S(1)} %copy-done.5, f32[1152,1]{1,0:T(8,128)S(1)} %copy-done.7), custom_call_target="tpu_custom_call" | custom-call | tf_op jit(solution)/shard_map/sources/pallas_call | solution.py:69
  63.8 0.0 copy-start.2
  63.8 0.8 copy-done.2
  64.6 12.8 %all_to_all.16 = f32[8,144,128]{2,1,0:T(8,128)S(1)} all-to-all(f32[8,144,128]{2,1,0:T(8,128)S(1)} %bitcast.49), channel_id=1, replica_groups=mesh['grid'=4,'space'=4,'spec'=2] {'space','spec'}, dimensions={0} | all-to-all | bytes 1179648 | tf_op jit(solution)/shard_map/all_to_all | solution.py:179
  77.4 0.2 fusion.6
  77.6 0.3 copy.53
  78.0 1.3 %collective-permute-start.3 = (f32[8,144]{1,0:T(8,128)S(1)}, f32[8,144]{1,0:T(8,128)S(1)}, u32[]{:S(2)}, u32[]{:S(2)}) collective-permute-start(f32[8,144]{1,0:T(8,128)S(1)} %bitcast.69), channel_id=1, source_target_pairs={{8,0},{16,8},{24,16},{9,1},{17,9},{25,17},{10,2},{18,10},{26,18},{... | collective-permute-start | bytes 13832 | tf_op jit(solution)/shard_map/ppermute | solution.py:151
  79.3 0.0 copy-done.3
  79.3 2.4 %fusion.7 = f32[128,128]{1,0:T(8,128)} fusion(f32[128,1152]{1,0:T(8,128)} %constant.40.clone, f32[1152,128]{1,0:T(8,128)S(1)} %copy-done.3), kind=kOutput, calls=%fused_computation.29 | convolution fusion | flops 226492416 | bytes 1245184 | tf_op jit(solution)/shard_map/dot_general | solution.py:269
  81.7 0.3 copy.52
  82.0 4.5 %collective-permute-start.2 = (f32[8,144]{1,0:T(8,128)S(1)}, f32[8,144]{1,0:T(8,128)S(1)}, u32[]{:S(2)}, u32[]{:S(2)}) collective-permute-start(f32[8,144]{1,0:T(8,128)S(1)} %bitcast.66), channel_id=1, source_target_pairs={{0,8},{8,16},{16,24},{1,9},{9,17},{17,25},{2,10},{10,18},{18,26},{... | collective-permute-start | bytes 13832 | tf_op jit(solution)/shard_map/ppermute | solution.py:151
  86.5 0.0 collective-permute-done.3
  86.5 0.6 gather_fusion.3
  87.1 0.1 broadcast_select_fusion
  87.2 0.1 reshape.96
  87.3 0.6 collective-permute-done.2
  87.9 0.6 gather_fusion.2
  88.5 0.1 broadcast_select_fusion.1
  88.5 0.1 reshape.95
  88.6 12.4 %propagate.3 = f32[144,8,128]{2,1,0:T(8,128)} custom-call(f32[2,144]{1,0:T(2,128)S(1)} %dynamic-slice_bitcast_fusion.refs_0_, f32[1152,128]{1,0:T(8,128)S(1)} %bitcast.48, f32[1440,128]{1,0:T(8,128)S(1)} %reshape_reshape_transpose_reshape.8.refs_1_.refs_2_, f32[8,8,128]{2,1,0:T(8,128)S(1)} %pad.15.refs_3_, f32[8,8,128]{2,1,0:T(8,128)S(1)} %pad.16.refs_4_, ...), custom_call_target="tpu_custom_call" | custom-call | tf_op jit(solution)/shard_map/propagate/pallas_call | solution.py:166
  (24 shorter events, 0.2 us)
Async XLA Ops:
  1.6 6.6 %copy-start.4 = (f32[1152,1]{1,0:T(8,128)}, f32[1152,1]{1,0:T(8,128)S(1)}, u32[]{:S(2)}) copy-start(f32[1152,1]{1,0:T(8,128)S(1)} %mul.31.refs_3_) | copy-start | bytes 13828
  2.5 5.7 %copy-start.6 = (f32[1152,1]{1,0:T(8,128)}, f32[1152,1]{1,0:T(8,128)S(1)}, u32[]{:S(2)}) copy-start(f32[1152,1]{1,0:T(8,128)S(1)} %reshape.143.refs_4_) | copy-start | bytes 13828
  4.3 1.7 %copy-start = (bf16[1152,1152]{1,0:T(8,128)(2,1)S(1)}, bf16[1152,1152]{1,0:T(8,128)(2,1)}, u32[]{:S(2)}) copy-start(bf16[1152,1152]{1,0:T(8,128)(2,1)} %refs_2_.3) | copy-start | bytes 7962628
  6.1 1.1 %copy-start.8 = (f32[1,32,36,1,128]{4,3,2,1,0:T(1,128)S(1)}, f32[1,32,36,1,128]{4,3,2,1,0:T(1,128)}, u32[]{:S(2)}) copy-start(f32[1,32,36,1,128]{4,3,2,1,0:T(1,128)} %param.15) | copy-start | bytes 1769476
  8.2 6.2 %copy-start.11 = (s32[1,8]{1,0:T(1,128)S(1)}, s32[1,8]{1,0:T(1,128)}, u32[]{:S(2)}) copy-start(s32[1,8]{1,0:T(1,128)} %param.17) | copy-start | bytes 100
  8.2 6.2 %copy-start.12 = (s32[1,8]{1,0:T(1,128)S(1)}, s32[1,8]{1,0:T(1,128)}, u32[]{:S(2)}) copy-start(s32[1,8]{1,0:T(1,128)} %param.18) | copy-start | bytes 100
  9.2 17.4 %all-to-all-start = ((f32[8,180,128]{2,1,0:T(8,128)}), f32[8,180,128]{2,1,0:T(8,128)S(1)}, u32[]{:S(2)}, u32[]{:S(2)}) async-start(f32[8,180,128]{2,1,0:T(8,128)} %pad_maximum_fusion), calls=%async_computation | async-start | bytes 1507328 | tf_op jit(solution)/shard_map/all_to_all | solution.py:179
  14.4 23.8 %copy-start.9 = (s32[1,8,128]{2,1,0:T(8,128)S(1)}, s32[1,8,128]{2,1,0:T(8,128)}, u32[]{:S(2)}) copy-start(s32[1,8,128]{2,1,0:T(8,128)} %param.16) | copy-start | bytes 12292
  26.6 5.1 %copy-start.10 = (f32[8,180,128]{2,1,0:T(8,128)}, f32[8,180,128]{2,1,0:T(8,128)S(1)}, u32[]{:S(2)}) copy-start(f32[8,180,128]{2,1,0:T(8,128)S(1)} %all-to-all-done) | copy-start | bytes 2211844
  27.2 7.3 %collective-permute-start = (f32[8,144]{1,0:T(8,128)S(1)}, f32[8,144]{1,0:T(8,128)S(1)}, u32[]{:S(2)}, u32[]{:S(2)}) collective-permute-start(f32[8,144]{1,0:T(8,128)S(1)} %bitcast.68), channel_id=1, source_target_pairs={{0,8},{8,16},{16,24},{1,9},{9,17},{17,25},{2,10},{10,18},{18,26},{... | collective-permute-start | bytes 13832 | tf_op jit(solution)/shard_map/ppermute | solution.py:151
  31.7 31.0 %copy-start.1 = (bf16[1152,1152]{1,0:T(8,128)(2,1)S(1)}, bf16[1152,1152]{1,0:T(8,128)(2,1)}, u32[]{:S(2)}) copy-start(bf16[1152,1152]{1,0:T(8,128)(2,1)} %refs_2_.3) | copy-start | bytes 7962628
  31.7 5.8 %collective-permute-start.1 = (f32[8,144]{1,0:T(8,128)S(1)}, f32[8,144]{1,0:T(8,128)S(1)}, u32[]{:S(2)}, u32[]{:S(2)}) collective-permute-start(f32[8,144]{1,0:T(8,128)S(1)} %bitcast.67), channel_id=1, source_target_pairs={{8,0},{16,8},{24,16},{9,1},{17,9},{25,17},{10,2},{18,10},{26,18},{... | collective-permute-start | bytes 13832 | tf_op jit(solution)/shard_map/ppermute | solution.py:151
  38.2 24.5 %copy-start.5 = (f32[1152,1]{1,0:T(8,128)S(1)}, f32[1152,1]{1,0:T(8,128)}, u32[]{:S(2)}) copy-start(f32[1152,1]{1,0:T(8,128)} %copy-done.4) | copy-start | bytes 13828
  38.2 24.5 %copy-start.7 = (f32[1152,1]{1,0:T(8,128)S(1)}, f32[1152,1]{1,0:T(8,128)}, u32[]{:S(2)}) copy-start(f32[1152,1]{1,0:T(8,128)} %copy-done.6) | copy-start | bytes 13828
  63.8 0.8 copy-start.2
  77.4 1.9 %copy-start.3 = (f32[1152,128]{1,0:T(8,128)S(1)}, f32[1152,128]{1,0:T(8,128)}, u32[]{:S(2)}) copy-start(f32[1152,128]{1,0:T(8,128)} %copy-done.2) | copy-start | bytes 1769476
  78.0 8.6 %collective-permute-start.3 = (f32[8,144]{1,0:T(8,128)S(1)}, f32[8,144]{1,0:T(8,128)S(1)}, u32[]{:S(2)}, u32[]{:S(2)}) collective-permute-start(f32[8,144]{1,0:T(8,128)S(1)} %bitcast.69), channel_id=1, source_target_pairs={{8,0},{16,8},{24,16},{9,1},{17,9},{25,17},{10,2},{18,10},{26,18},{... | collective-permute-start | bytes 13832 | tf_op jit(solution)/shard_map/ppermute | solution.py:151
  82.0 5.9 %collective-permute-start.2 = (f32[8,144]{1,0:T(8,128)S(1)}, f32[8,144]{1,0:T(8,128)S(1)}, u32[]{:S(2)}, u32[]{:S(2)}) collective-permute-start(f32[8,144]{1,0:T(8,128)S(1)} %bitcast.66), channel_id=1, source_target_pairs={{0,8},{8,16},{16,24},{1,9},{9,17},{17,25},{2,10},{10,18},{18,26},{... | collective-permute-start | bytes 13832 | tf_op jit(solution)/shard_map/ppermute | solution.py:151
where the time goes:
time: 102 us; the launch traced here: 101 us
  Pallas kernels  26.1 us (26%)
  blocking collectives  25.7 us (25%)
  starting transfers between devices  16 us (16%)
  waiting for transfers between devices  15.1 us (15%)
  local copies, waits for them, and re-layouts  11.1 us (11%)
  matrix products  3.45 us (3%)
  other arithmetic  2.71 us (3%)
    all_to_all x2, blocking collectives, exchange(): lax.all_to_all(payload, ('space', 'spec'), split_axis=0, concat_axis=0, t...  25.7 us
    pallas_call x2, Pallas kernels, propagate(): pl.pallas_call(functools.partial(sweep_kernel, rows, dirs, freqs, held, f...  24 us
    all_to_all x1, waiting for transfers between devices, exchange(): lax.all_to_all(payload, ('space', 'spec'), split_axis=0, concat_axis=0, t...  12.1 us
    ppermute x4, starting transfers between devices, neighbour(): return lax.ppermute(column, 'grid', route)  10.9 us
    all_to_all x1, starting transfers between devices, exchange(): lax.all_to_all(payload, ('space', 'spec'), split_axis=0, concat_axis=0, t...  5.17 us
    unnamed x30, local copies, waits for them, and re-layouts  4.99 us
    ppermute x4, waiting for transfers between devices, neighbour(): return lax.ppermute(column, 'grid', route)  2.93 us
    dot_general x1, matrix products, shards(): stokes = jnp.dot(stokes_table, spectra, precision=highest)  2.39 us
  transfers between devices with their start and end apart: 5, of which 3 were waited for; matrix products, arithmetic and copies ran while one was open for 6% of the time, Pallas kernels for 0%

commit v1 on v0

v1 whole, which is shorter than its diff:
```python
import functools
import math

import jax
import jax.numpy as jnp
import numpy as np
from jax import lax
from jax.experimental import pallas as pl
from jax.experimental.pallas import tpu as pltpu
from jax.sharding import PartitionSpec as P

sigma_base = 0.2199
gravity = 9.81
growth = 1.1
courant_scale = 3.0
time_step = 0.5
stokes_gain = 2.0
highest = lax.Precision.HIGHEST
mesh_ids = pl.DeviceIdType.MESH
vmem = pl.BlockSpec(memory_space=pltpu.VMEM)
smem = pl.BlockSpec(memory_space=pltpu.SMEM)
anywhere = pl.BlockSpec(memory_space=pl.ANY)


def tables(freq_count, directions, levels):
    freq_steps = np.arange(freq_count).astype(np.float64)
    radian_freq = sigma_base * growth**freq_steps
    wavenum = radian_freq * radian_freq / gravity
    angles = 2.0 * np.pi * np.arange(directions) / directions
    depths = -(np.arange(levels) + 0.5)
    decays = np.exp(2.0 * wavenum[:, None] * depths[None, :])
    current_weight = decays / np.sum(decays, axis=1, keepdims=True)
    drifts = (radian_freq * wavenum)[:, None] * decays
    drifts = drifts / np.sum(drifts, axis=0, keepdims=True)
    return (angles, current_weight.astype(np.float32), drifts)


def wave_kernel(
    ranks,
    cores,
    dirs,
    freqs,
    chunks,
    tile,
    spectrum_ref,
    sea_own_ref,
    sea_ref,
    west_order,
    east_order,
    u_ref,
    v_ref,
    weight_ref,
    gain_ref,
    damping_ref,
    courant_ref,
    transfer_hbm,
    drift_hbm,
    waves_ref,
    stokes_ref,
    transfer_ref,
    drift_ref,
    held,
    flow_send,
    flow_recv,
    flow_x,
    flow_y,
    send,
    recv,
    edge_send,
    west_first,
    east_first,
    west_second,
    east_second,
    order,
    ghosts,
    load_sem,
    send_sem,
    recv_sem,
    flow_send_sem,
    flow_recv_sem,
    edge_send_sem,
    edge_recv_sem,
):
    edge_recv = ((west_first, east_first), (west_second, east_second))
    groups = ranks * cores
    padded = send.shape[2]
    piece = padded // chunks
    rows = recv.shape[1]
    columns = recv.shape[3]
    freq_count = cores * freqs
    plane, planes = lax.axis_index("grid"), lax.axis_size("grid")
    space = lax.axis_index("space")
    me = space * cores + lax.axis_index("spec")
    has_west, has_east = plane > 0, plane < planes - 1
    sides = ((0, has_east, has_west, plane + 1), (1, has_west, has_east, plane - 1))

    def device(level, block):
        return (level, block // cores, block % cores)

    loads = [
        pltpu.make_async_copy(transfer_hbm, transfer_ref, load_sem.at[0]),
        pltpu.make_async_copy(drift_hbm, drift_ref, load_sem.at[1]),
    ]
    for load in loads:
        load.start()

    barrier = pltpu.get_barrier_semaphore()
    for k in range(1, groups):
        partner = device(plane, lax.rem(me + k, groups))
        pl.semaphore_signal(barrier, inc=1, device_id=partner, device_id_type=mesh_ids)
    for _, exists, _, level in sides:

        @pl.when(exists)
        def _():
            for g in range(groups):
                pl.semaphore_signal(
                    barrier, inc=1, device_id=device(level, g), device_id_type=mesh_ids
                )

    def flow_copy(k):
        partner = lax.rem(me + k, groups)
        return pltpu.make_async_remote_copy(
            src_ref=flow_send.at[partner % cores],
            dst_ref=flow_recv.at[me],
            send_sem=flow_send_sem.at[k],
            recv_sem=flow_recv_sem.at[k],
            device_id=device(plane, partner),
            device_id_type=mesh_ids,
        )

    def piece_copy(phase, ch, k):
        partner = lax.rem(me + k, groups)
        part = pl.ds(pl.multiple_of(ch * piece, 8), piece)
        return pltpu.make_async_remote_copy(
            src_ref=send.at[phase, partner, part],
            dst_ref=recv.at[phase, me, part],
            send_sem=send_sem.at[phase, ch, k],
            recv_sem=recv_sem.at[phase, ch, k],
            device_id=device(plane, partner),
            device_id_type=mesh_ids,
        )

    def arrival(phase, ch, k):
        source = lax.rem(me + groups - k, groups)
        part = pl.ds(pl.multiple_of(ch * piece, 8), piece)
        return pltpu.make_async_remote_copy(
            src_ref=send.at[phase, source, part],
            dst_ref=recv.at[phase, source, part],
            send_sem=send_sem.at[phase, ch, k],
            recv_sem=recv_sem.at[phase, ch, k],
            device_id=device(plane, source),
            device_id_type=mesh_ids,
        )

    def edge_copy(stage, side, level, g, rank):
        return pltpu.make_async_remote_copy(
            src_ref=edge_send.at[stage, g],
            dst_ref=edge_recv[stage][side].at[rank],
            send_sem=edge_send_sem.at[stage, side, g],
            recv_sem=edge_recv_sem.at[stage, side, rank],
            device_id=device(level, g),
            device_id_type=mesh_ids,
        )

    for at, current in ((0, u_ref), (1, v_ref)):
        flow = jnp.dot(
            weight_ref[...], current[...], precision=highest, preferred_element_type=jnp.float32
        )
        for c in range(cores):
            flow_send[c, at * freqs : (at + 1) * freqs, :] = flow[c * freqs : (c + 1) * freqs]

    planes_beside = jnp.minimum(plane, 1) + jnp.minimum(planes - 1 - plane, 1)
    pl.semaphore_wait(barrier, groups - 1 + groups * planes_beside)

    for k in range(1, groups):
        flow_copy(k).start()
    flow_recv[me] = flow_send[lax.axis_index("spec")]

    natural = [
        (s * cores + c, d, (s * dirs + d) * freq_count + c * freqs)
        for s in range(ranks)
        for d in range(dirs)
        for c in range(cores)
    ]
    lane8 = lax.broadcasted_iota(jnp.int32, (8, columns), 1)
    row8 = lax.broadcasted_iota(jnp.int32, (8, columns), 0)
    ends = (row8 == 0) & (lane8 == columns - 1) | (row8 == 1) & (lane8 == 0)
    ends = ends.astype(jnp.float32)

    def sources(stage, spectra):
        phase = 2 * stage
        redist = jnp.dot(
            transfer_ref[...], spectra.astype(jnp.bfloat16), preferred_element_type=jnp.float32
        )
        energy = jnp.sum(spectra * spectra, axis=0, keepdims=True) * (1.0 / spectra.shape[0])
        held[...] = (
            sea_own_ref[...]
            * (spectra * (1.0 + time_step * gain_ref[...]) + time_step * redist)
            / (1.0 + time_step * damping_ref[...] * energy)
        )
        for g, d, here in natural:
            send[phase, g, pl.ds(d, freqs, stride=dirs), :] = held[here : here + freqs, :]
        for k in range(1, groups):
            piece_copy(phase, 0, k).start()
        for g in range(groups):
            edge_send[stage, g, :, :padded] = lax.dot_general(
                ends,
                send[phase, g],
                (((1,), (1,)), ((), ())),
                precision=highest,
                preferred_element_type=jnp.float32,
            )
        for side, exists, _, level in sides:

            @pl.when(exists)
            def _():
                for g in range(groups):
                    edge_copy(stage, side, level, g, me).start()

        for ch in range(1, chunks):
            for k in range(1, groups):
                piece_copy(phase, ch, k).start()
        recv[phase, me] = send[phase, me]

    def border(stage):
        for side, _, exists, level in sides:
            wanted = (west_order, east_order)[side]

            @pl.when(exists)
            def _():
                for r in range(groups):
                    edge_copy(stage, side, level, r, r).wait_recv()
                order[...] = jnp.zeros_like(order)
                for y in range(rows):
                    order[y : y + 1, :] = edge_recv[stage][side][wanted[y], side : side + 1, :]
                square = (padded, padded)
                unit = lax.broadcasted_iota(jnp.int32, square, 0) == lax.broadcasted_iota(
                    jnp.int32, square, 1
                )
                ghosts[side] = lax.dot_general(
                    unit.astype(jnp.float32),
                    order[:, :padded],
                    (((1,), (1,)), ((), ())),
                    precision=highest,
                    preferred_element_type=jnp.float32,
                )

            @pl.when(jnp.logical_not(exists))
            def _():
                ghosts[side] = jnp.zeros(ghosts.shape[1:], jnp.float32)

    shape = (tile, columns)
    lane = lax.broadcasted_iota(jnp.int32, shape, 1)
    first, last = lane == 0, lane == columns - 1
    quadrant = (space * dirs) // (ranks * dirs // 4)
    onward = (quadrant == 0) | (quadrant == 3)
    ahead = onward.astype(jnp.int32)
    place = ahead * lane + (1 - ahead) * (columns - 1 - lane)

    def rolled(block, turn):
        flat = pltpu.roll(block.reshape(-1, columns), turn, 1)
        return flat.reshape(block.shape)

    def sweep(phase, base):
        part = pl.ds(pl.multiple_of(base, 8), tile)
        wave = recv[phase, :, part, :]
        a, b = flow_x[:, part, :], flow_y[:, part, :]
        cx = jnp.broadcast_to(courant_ref[0, part, :], shape)
        cy = jnp.broadcast_to(courant_ref[1, part, :], shape)
        raw_west, raw_east = ghosts[0, part, :], ghosts[1, part, :]
        ghost_west = jnp.stack(
            [
                jnp.where(first, pltpu.roll(raw_west, (columns - y) % columns, 1), 0.0)
                for y in range(rows)
            ]
        )
        ghost_east = jnp.stack(
            [
                jnp.where(last, pltpu.roll(raw_east, columns - 1 - y, 1), 0.0)
                for y in range(rows)
            ]
        )
        blank = jnp.zeros((1,) + shape, jnp.float32)
        west = jnp.where(first[None], ghost_west, rolled(wave, 1))
        east = jnp.where(last[None], ghost_east, rolled(wave, columns - 1))
        north = jnp.concatenate([blank, wave[:-1]], axis=0)
        south = jnp.concatenate([wave[1:], blank], axis=0)
        moved = (
            wave
            - jnp.maximum(a, 0.0) * (wave - west)
            - jnp.maximum(-a, 0.0) * (wave - east)
            - jnp.maximum(b, 0.0) * (wave - north)
            - jnp.maximum(-b, 0.0) * (wave - south)
            + jnp.maximum(cx, 0.0)[None] * ghost_west
            + jnp.maximum(-cx, 0.0)[None] * ghost_east
        )
        speed = jnp.abs(cx)
        scale = 1.0 / (1.0 + speed)
        ratio = speed * scale
        swept = moved * scale[None]
        step = 1
        while step < columns:
            turn = ahead * step + (1 - ahead) * (columns - step)
            swept = swept + jnp.where(place >= step, ratio, 0.0)[None] * rolled(swept, turn)
            ratio = ratio * ratio
            step *= 2
        scale = 1.0 / (1.0 + jnp.abs(cy))
        down, up = jnp.maximum(cy, 0.0) * scale, jnp.maximum(-cy, 0.0) * scale
        lines = [swept[y] * scale for y in range(rows)]
        for y in range(1, rows):
            lines[y] = lines[y] + down * lines[y - 1]
        for y in range(rows - 2, -1, -1):
            lines[y] = lines[y] + up * lines[y + 1]
        return [sea_ref[y : y + 1, :].astype(jnp.float32) * lines[y] for y in range(rows)]

    def propagate(phase, emit, after):
        def chunk(ch, carry):
            for k in range(1, groups):
                arrival(phase, ch, k).wait_recv()
            for t in range(piece // tile):
                base = ch * piece + t * tile
                emit(base, sweep(phase, base))
            after(ch)
            return carry

        lax.fori_loop(0, chunks, chunk, 0)

    def emit_send(base, lines):
        for y in range(rows):
            send[1, y, pl.ds(pl.multiple_of(base, 8), tile), :] = lines[y]

    def send_piece(ch):
        for k in range(1, groups):
            piece_copy(1, ch, k).start()
        part = pl.ds(pl.multiple_of(ch * piece, 8), piece)
        recv[1, me, part, :] = send[1, me, part, :]

    def emit_waves(base, lines):
        freq = base // dirs
        for y in range(rows):
            for f in range(min(tile // dirs, freqs)):
                waves_ref[pl.ds((freq + f) * rows + y, dirs, stride=freqs * rows), :] = lines[y][
                    f * dirs : (f + 1) * dirs
                ]

    loads[0].wait()
    sources(0, spectrum_ref[...])
    for k in range(1, groups):
        source = lax.rem(me + groups - k, groups)
        pltpu.make_async_remote_copy(
            src_ref=flow_send.at[0],
            dst_ref=flow_recv.at[source],
            send_sem=flow_send_sem.at[k],
            recv_sem=flow_recv_sem.at[k],
            device_id=device(plane, source),
            device_id_type=mesh_ids,
        ).wait_recv()
    for f in range(freqs):
        wide = (rows, dirs, columns)
        flow_x[:, f * dirs : (f + 1) * dirs, :] = jnp.broadcast_to(
            flow_recv[:, f : f + 1, :], wide
        )
        flow_y[:, f * dirs : (f + 1) * dirs, :] = jnp.broadcast_to(
            flow_recv[:, freqs + f : freqs + f + 1, :], wide
        )
    border(0)
    propagate(0, emit_send, send_piece)
    for k in range(1, groups):
        for ch in range(chunks):
            arrival(1, ch, k).wait_recv()
    for g, d, here in natural:
        held[here : here + freqs, :] = recv[1, g, pl.ds(d, freqs, stride=dirs), :]
    sources(1, held[...])
    loads[1].wait()
    stokes_ref[...] = jnp.dot(
        drift_ref[...], held[...], precision=highest, preferred_element_type=jnp.float32
    )
    border(1)
    propagate(2, emit_waves, lambda ch: None)

    for k in range(1, groups):
        flow_copy(k).wait_send()
        for phase in range(3):
            for ch in range(chunks):
                piece_copy(phase, ch, k).wait_send()
    for stage in range(2):
        for side, exists, _, level in sides:

            @pl.when(exists)
            def _():
                for g in range(groups):
                    edge_copy(stage, side, level, g, me).wait_send()


def rounded_up(count, unit):
    return -(-count // unit) * unit


def shards(
    spectrum,
    land_sea,
    west_index,
    east_index,
    current_u,
    current_v,
    transfer,
    wind_rate,
    dissipation,
):
    ranks = lax.axis_size("space")
    cores = lax.axis_size("spec")
    directions, freq_count, rows_local, columns = spectrum.shape[1:]
    levels = current_u.shape[1]
    total_rows = land_sea.shape[1]
    dir_local = directions // ranks
    freq_local = freq_count // cores
    components = directions * freq_count
    comps_local = dir_local * freq_local
    groups = ranks * cores
    padded = rounded_up(comps_local, 8)
    tile = 24 if padded % 24 == 0 else 8
    chunks = 3 if padded % (3 * tile) == 0 else 1
    width = rounded_up(padded, 128)
    flow_rows = rounded_up(2 * freq_local, 8)
    space_rank = lax.axis_index("space")
    core_rank = lax.axis_index("spec")
    block_rank = space_rank * cores + core_rank
    angles, current_weight, drifts = tables(freq_count, directions, levels)
    cosines, sines = np.cos(angles), np.sin(angles)
    cosines[np.abs(cosines) < 1e-12] = 0.0
    sines[np.abs(sines) < 1e-12] = 0.0
    speeds = courant_scale * growth ** (-np.arange(freq_count).astype(np.float64))
    courant = np.stack([cosines[:, None] * speeds[None, :], sines[:, None] * speeds[None, :]])
    courant = courant.reshape(2, ranks, dir_local, cores, freq_local).transpose(1, 3, 0, 4, 2)
    courant = courant.reshape(groups, 2, comps_local, 1).astype(np.float32)
    courant = np.pad(courant, ((0, 0), (0, 0), (0, padded - comps_local), (0, 0)))
    courant = lax.dynamic_index_in_dim(jnp.asarray(courant), block_rank, 0, keepdims=False)

    trig = np.stack([cosines, sines]) * stokes_gain / math.sqrt(directions)
    stokes_table = trig[:, None, :, None] * drifts.T[None, :, None, :]
    stokes_table = stokes_table.reshape(2 * levels, components).astype(np.float32)

    heading = jnp.asarray((0.5 * (1.0 + cosines)).astype(np.float32))
    gain = (heading[:, None] * wind_rate[None, :]).reshape(components, 1)
    damping = jnp.broadcast_to(dissipation[None, :], (directions, freq_count))
    damping = damping.reshape(components, 1)
    sea_own = lax.dynamic_slice_in_dim(land_sea[0], block_rank, 1, 0).astype(jnp.float32)
    f32 = jnp.float32
    waves, stokes = pl.pallas_call(
        functools.partial(
            wave_kernel, ranks, cores, dir_local, freq_local, chunks, tile
        ),
        out_shape=(
            jax.ShapeDtypeStruct((comps_local * total_rows, columns), f32),
            jax.ShapeDtypeStruct((2 * levels, columns), f32),
        ),
        in_specs=[vmem] * 3 + [smem] * 2 + [vmem] * 6 + [anywhere] * 2,
        out_specs=(vmem, vmem),
        scratch_shapes=[
            pltpu.VMEM(transfer.shape, transfer.dtype),
            pltpu.VMEM(stokes_table.shape, f32),
            pltpu.VMEM((components, columns), f32),
            pltpu.VMEM((cores, flow_rows, columns), f32),
            pltpu.VMEM((groups, flow_rows, columns), f32),
            pltpu.VMEM((groups, padded, columns), f32),
            pltpu.VMEM((groups, padded, columns), f32),
            pltpu.VMEM((3, groups, padded, columns), f32),
            pltpu.VMEM((3, groups, padded, columns), f32),
            pltpu.VMEM((2, groups, 8, width), f32),
            pltpu.VMEM((groups, 8, width), f32),
            pltpu.VMEM((groups, 8, width), f32),
            pltpu.VMEM((groups, 8, width), f32),
            pltpu.VMEM((groups, 8, width), f32),
            pltpu.VMEM((columns, width), f32),
            pltpu.VMEM((2, padded, columns), f32),
            pltpu.SemaphoreType.DMA((2,)),
            pltpu.SemaphoreType.DMA((3, chunks, groups)),
            pltpu.SemaphoreType.DMA((3, chunks, groups)),
            pltpu.SemaphoreType.DMA((groups,)),
            pltpu.SemaphoreType.DMA((groups,)),
            pltpu.SemaphoreType.DMA((2, 2, groups)),
            pltpu.SemaphoreType.DMA((2, 2, groups)),
        ],
        compiler_params=pltpu.CompilerParams(
            collective_id=0, has_side_effects=True, vmem_limit_bytes=48 * 1024 * 1024
        ),
        name="waves",
    )(
        spectrum[0].reshape(components, columns),
        sea_own,
        land_sea[0],
        west_index[0],
        east_index[0],
        current_u[0].reshape(levels, columns),
        current_v[0].reshape(levels, columns),
        jnp.asarray(current_weight),
        gain,
        damping,
        courant,
        transfer,
        jnp.asarray(stokes_table),
    )
    return (
        waves.reshape(1, dir_local, freq_local, total_rows, columns),
        stokes.reshape(1, 2 * levels, rows_local, columns),
    )


def solution(mesh):
    placed = (
        P("grid", None, None, ("space", "spec"), None),
        P("grid", None, None),
        P("grid", None),
        P("grid", None),
        P("grid", None, ("space", "spec"), None),
        P("grid", None, ("space", "spec"), None),
        P(),
        P(),
        P(),
    )
    return jax.shard_map(
        shards,
        mesh=mesh,
        in_specs=placed,
        out_specs=(
            P("grid", "space", "spec", None, None),
            P("grid", None, ("space", "spec"), None),
        ),
        check_vma=False,
    )
```

time: 102 us -> 51 us (0.50)
  blocking collectives: 25.7 us -> 0 us
  starting transfers between devices: 16 us -> 0 us
  waiting for transfers between devices: 15.1 us -> 0 us
  Pallas kernels: 26.1 us -> 36.7 us
  matrix products: 3.45 us -> 0 us
  other arithmetic: 2.71 us -> 1.44 us
    all_to_all x2 -> x0, blocking collectives: 25.7 us -> none  [exchange(): lax.all_to_all(payload, ('space', 'spec'), split_axis=0, concat_axis=0, t...]
    all_to_all x1 -> x0, waiting for transfers between devices: 12.1 us -> none  [exchange(): lax.all_to_all(payload, ('space', 'spec'), split_axis=0, concat_axis=0, t...]
    ppermute x4 -> x0, starting transfers between devices: 10.9 us -> none  [neighbour(): return lax.ppermute(column, 'grid', route)]
    pallas_call x4 -> x1, Pallas kernels: 26.1 us -> 36.7 us  [shards(): pl.pallas_call(functools.partial(wave_kernel, ranks, cores, dir_local, fr...]
    all_to_all x1 -> x0, starting transfers between devices: 5.17 us -> none  [exchange(): lax.all_to_all(payload, ('space', 'spec'), split_axis=0, concat_axis=0, t...]
    unnamed x30 -> x20, local copies, waits for them, and re-layouts: 4.99 us -> 9.56 us
    dot_general x2 -> x0, matrix products: 3.45 us -> none  [the longest x1 2.39 us: shards(): stokes = jnp.dot(stokes_table, spectra, precision=highest)]
    ppermute x4 -> x0, waiting for transfers between devices: 2.93 us -> none  [neighbour(): return lax.ppermute(column, 'grid', route)]
  transfers between devices with their start and end apart: 5 -> 0, of which waited for: 3 -> 0; matrix products, arithmetic and copies ran while one was open for 6% -> 0% of each run, Pallas kernels for 0% -> 0%
where the time goes in v1:
time: 51 us; the launch traced here: 50.3 us
  Pallas kernels  36.7 us (72%)
  local copies, waits for them, and re-layouts  11.5 us (23%)
  other arithmetic  1.44 us (3%)
  between operations  0.67 us (1%)
    pallas_call x1, Pallas kernels, shards(): pl.pallas_call(functools.partial(wave_kernel, ranks, cores, dir_local, fr...  36.7 us
    unnamed x20, local copies, waits for them, and re-layouts  9.56 us

profile of v1, /device:TPU:0, one launch (start us, length us, event | category | flops | bytes accessed | tf_op | source)
XLA Modules:
  0.0 50.3 jit_solution(3178115316726239582)
XLA Ops:
  0.6 0.7 %convert_bitcast_fusion.sea_own_ref = f32[1,128]{1,0:T(1,128)S(1)} fusion(s32[1,8,128]{2,1,0:T(8,128)} %param.14, s32[]{:T(128)S(6)} %select_n.5), kind=kLoop, calls=%fused_computation.2 | loop fusion | flops 128 | bytes 1028 | tf_op jit(solution)/shard_map/convert_element_type | solution.py:447
  1.3 0.7 %dynamic-slice_bitcast_fusion = f32[2,144,1]{1,0,2:T(2,128)S(1)} fusion(f32[8,2,144,1]{2,1,3,0:T(2,128)} %constant.27.clone, s32[]{:T(128)S(6)} %select_n.5), kind=kLoop, calls=%fused_computation.1 | loop fusion | bytes 2308 | tf_op jit(solution)/shard_map/jit(dynamic_index_in_dim)/squeeze | solution.py:437
  2.0 0.7 %broadcast_multiply_fusion = f32[32,36]{1,0:T(8,128)S(1)} fusion(f32[36]{0:T(128)} %param.20, f32[32]{0:T(128)} %constant.28.clone), kind=kLoop, calls=%fused_computation | loop fusion | flops 1152 | bytes 4880 | tf_op jit(solution)/shard_map/mul | solution.py:444
  2.8 0.7 %broadcast_in_dim.2 = f32[32,36]{1,0:T(8,128)S(1)} broadcast(f32[36]{0:T(128)} %param.21), dimensions={1} | broadcast | bytes 4752 | tf_op jit(solution)/shard_map/broadcast_in_dim | solution.py:445
  3.4 0.1 copy.18.courant_ref
  3.6 0.2 reshape.56.damping_ref
  3.8 0.2 mul.31.gain_ref
  4.0 0.0 copy-start
  4.0 1.7 %copy-done = bf16[1152,1152]{1,0:T(8,128)(2,1)S(1)} copy-done((bf16[1152,1152]{1,0:T(8,128)(2,1)S(1)}, bf16[1152,1152]{1,0:T(8,128)(2,1)}, u32[]{:S(2)}) %copy-start) | copy-done | bytes 2654232
  5.7 0.0 copy-start.1
  5.7 1.1 %copy-done.1 = f32[1,32,36,1,128]{4,3,2,1,0:T(1,128)S(1)} copy-done((f32[1,32,36,1,128]{4,3,2,1,0:T(1,128)S(1)}, f32[1,32,36,1,128]{4,3,2,1,0:T(1,128)}, u32[]{:S(2)}) %copy-start.1) | copy-done | bytes 589848
  6.8 0.0 copy-start.2
  6.8 1.1 %copy-done.2 = f32[128,1152]{1,0:T(8,128)S(1)} copy-done((f32[128,1152]{1,0:T(8,128)S(1)}, f32[128,1152]{1,0:T(8,128)}, u32[]{:S(2)}) %copy-start.2) | copy-done | bytes 589848
  7.9 0.0 copy-start.3
  7.9 0.8 %copy-done.3 = f32[1,64,1,128]{3,2,1,0:T(1,128)S(1)} copy-done((f32[1,64,1,128]{3,2,1,0:T(1,128)S(1)}, f32[1,64,1,128]{3,2,1,0:T(1,128)}, u32[]{:S(2)}) %copy-start.3) | copy-done | bytes 32792
  8.6 0.0 copy-start.4
  8.6 0.8 %copy-done.4 = f32[1,64,1,128]{3,2,1,0:T(1,128)S(1)} copy-done((f32[1,64,1,128]{3,2,1,0:T(1,128)S(1)}, f32[1,64,1,128]{3,2,1,0:T(1,128)}, u32[]{:S(2)}) %copy-start.4) | copy-done | bytes 32792
  9.4 0.0 copy-start.5
  9.4 0.7 %copy-done.5 = f32[36,64]{1,0:T(8,128)S(1)} copy-done((f32[36,64]{1,0:T(8,128)S(1)}, f32[36,64]{1,0:T(8,128)}, u32[]{:S(2)}) %copy-start.5) | copy-done | bytes 9240
  10.1 0.0 copy-start.6
  10.1 0.7 %copy-done.6 = s32[1,8,128]{2,1,0:T(8,128)S(1)} copy-done((s32[1,8,128]{2,1,0:T(8,128)S(1)}, s32[1,8,128]{2,1,0:T(8,128)}, u32[]{:S(2)}) %copy-start.6) | copy-done | bytes 4120
  10.8 0.0 copy-start.7
  10.8 0.7 %copy-done.7 = s32[1,8]{1,0:T(1,128)S(1)} copy-done((s32[1,8]{1,0:T(1,128)S(1)}, s32[1,8]{1,0:T(1,128)}, u32[]{:S(2)}) %copy-start.7) | copy-done | bytes 56
  11.5 0.0 copy-start.8
  11.5 0.7 %copy-done.8 = s32[1,8]{1,0:T(1,128)S(1)} copy-done((s32[1,8]{1,0:T(1,128)S(1)}, s32[1,8]{1,0:T(1,128)}, u32[]{:S(2)}) %copy-start.8) | copy-done | bytes 56
  12.1 36.7 %waves.1 = (f32[1152,128]{1,0:T(8,128)S(1)}, f32[128,128]{1,0:T(8,128)S(1)}) custom-call(f32[1152,128]{1,0:T(8,128)S(1)} %bitcast.14, f32[1,128]{1,0:T(1,128)S(1)} %convert_bitcast_fusion.sea_own_ref, s32[8,128]{1,0:T(8,128)S(1)} %bitcast.19, s32[8]{0:T(128)S(1)} %bitcast.20, s32[8]{0:T(128)S(1)} %bitcast.21, f32[64,128]{1,0:T(8,128)S(1)} %bitcast.17, ...), custom_call_target="tpu_custom_call" | custom-call | tf_op jit(solution)/shard_map/waves/pallas_call | solution.py:449
  48.8 0.8 %copy.22 = f32[1,8,18,8,128]{4,3,2,1,0:T(8,128)} copy(f32[1,8,18,8,128]{4,3,2,1,0:T(8,128)S(1)} %bitcast.15) | data formatting | bytes 1179648
  49.6 0.6 %copy.23 = f32[1,128,1,128]{3,2,1,0:T(1,128)} copy(f32[1,128,1,128]{3,2,1,0:T(1,128)S(1)} %bitcast.16) | data formatting | bytes 131072
Async XLA Ops:
  4.0 1.8 %copy-start = (bf16[1152,1152]{1,0:T(8,128)(2,1)S(1)}, bf16[1152,1152]{1,0:T(8,128)(2,1)}, u32[]{:S(2)}) copy-start(bf16[1152,1152]{1,0:T(8,128)(2,1)} %transfer_hbm.1) | copy-start | bytes 7962628
  5.7 1.1 %copy-start.1 = (f32[1,32,36,1,128]{4,3,2,1,0:T(1,128)S(1)}, f32[1,32,36,1,128]{4,3,2,1,0:T(1,128)}, u32[]{:S(2)}) copy-start(f32[1,32,36,1,128]{4,3,2,1,0:T(1,128)} %param.13) | copy-start | bytes 1769476
  6.8 1.1 %copy-start.2 = (f32[128,1152]{1,0:T(8,128)S(1)}, f32[128,1152]{1,0:T(8,128)}, u32[]{:S(2)}) copy-start(f32[128,1152]{1,0:T(8,128)} %constant.30.clone.drift_hbm) | copy-start | bytes 1769476
  7.9 0.8 %copy-start.3 = (f32[1,64,1,128]{3,2,1,0:T(1,128)S(1)}, f32[1,64,1,128]{3,2,1,0:T(1,128)}, u32[]{:S(2)}) copy-start(f32[1,64,1,128]{3,2,1,0:T(1,128)} %param.17) | copy-start | bytes 98308
  8.6 0.8 %copy-start.4 = (f32[1,64,1,128]{3,2,1,0:T(1,128)S(1)}, f32[1,64,1,128]{3,2,1,0:T(1,128)}, u32[]{:S(2)}) copy-start(f32[1,64,1,128]{3,2,1,0:T(1,128)} %param.18) | copy-start | bytes 98308
  9.4 0.7 %copy-start.5 = (f32[36,64]{1,0:T(8,128)S(1)}, f32[36,64]{1,0:T(8,128)}, u32[]{:S(2)}) copy-start(f32[36,64]{1,0:T(8,128)} %constant.29.clone.weight_ref) | copy-start | bytes 27652
  10.1 0.7 %copy-start.6 = (s32[1,8,128]{2,1,0:T(8,128)S(1)}, s32[1,8,128]{2,1,0:T(8,128)}, u32[]{:S(2)}) copy-start(s32[1,8,128]{2,1,0:T(8,128)} %param.14) | copy-start | bytes 12292
  10.8 0.7 %copy-start.7 = (s32[1,8]{1,0:T(1,128)S(1)}, s32[1,8]{1,0:T(1,128)}, u32[]{:S(2)}) copy-start(s32[1,8]{1,0:T(1,128)} %param.15) | copy-start | bytes 100
  11.5 0.7 %copy-start.8 = (s32[1,8]{1,0:T(1,128)S(1)}, s32[1,8]{1,0:T(1,128)}, u32[]{:S(2)}) copy-start(s32[1,8]{1,0:T(1,128)} %param.16) | copy-start | bytes 100

commit v2 on v1

--- a/solution.py
+++ b/solution.py
@@ -18,8 +18,7 @@
 highest = lax.Precision.HIGHEST
 mesh_ids = pl.DeviceIdType.MESH
 vmem = pl.BlockSpec(memory_space=pltpu.VMEM)
-smem = pl.BlockSpec(memory_space=pltpu.SMEM)
-anywhere = pl.BlockSpec(memory_space=pl.ANY)
+in_place = pl.BlockSpec(memory_space=pltpu.HBM)
 
 
 def tables(freq_count, directions, levels):
@@ -42,23 +41,36 @@
     freqs,
     chunks,
     tile,
-    spectrum_ref,
-    sea_own_ref,
-    sea_ref,
-    west_order,
-    east_order,
+    u_hbm,
+    v_hbm,
+    weight_hbm,
+    wind_hbm,
+    dissipation_hbm,
+    spread_hbm,
+    spectrum_hbm,
+    transfer_hbm,
+    sea_hbm,
+    courant_hbm,
+    west_hbm,
+    east_hbm,
+    drift_hbm,
+    waves_ref,
+    stokes_ref,
     u_ref,
     v_ref,
     weight_ref,
+    wind_ref,
+    dissipation_ref,
+    spread_ref,
+    spectrum_ref,
+    transfer_ref,
+    sea_ref,
+    courant_ref,
+    west_order,
+    east_order,
+    drift_ref,
     gain_ref,
     damping_ref,
-    courant_ref,
-    transfer_hbm,
-    drift_hbm,
-    waves_ref,
-    stokes_ref,
-    transfer_ref,
-    drift_ref,
     held,
     flow_send,
     flow_recv,
@@ -97,13 +109,6 @@
     def device(level, block):
         return (level, block // cores, block % cores)
 
-    loads = [
-        pltpu.make_async_copy(transfer_hbm, transfer_ref, load_sem.at[0]),
-        pltpu.make_async_copy(drift_hbm, drift_ref, load_sem.at[1]),
-    ]
-    for load in loads:
-        load.start()
-
     barrier = pltpu.get_barrier_semaphore()
     for k in range(1, groups):
         partner = device(plane, lax.rem(me + k, groups))
@@ -116,6 +121,29 @@
                 pl.semaphore_signal(
                     barrier, inc=1, device_id=device(level, g), device_id_type=mesh_ids
                 )
+
+    loads = [
+        pltpu.make_async_copy(source, target, load_sem.at[i])
+        for i, (source, target) in enumerate(
+            (
+                (u_hbm, u_ref),
+                (v_hbm, v_ref),
+                (weight_hbm, weight_ref),
+                (wind_hbm, wind_ref),
+                (dissipation_hbm, dissipation_ref),
+                (spread_hbm, spread_ref),
+                (spectrum_hbm, spectrum_ref),
+                (transfer_hbm, transfer_ref),
+                (sea_hbm, sea_ref),
+                (courant_hbm.at[me], courant_ref),
+                (west_hbm, west_order),
+                (east_hbm, east_order),
+                (drift_hbm, drift_ref),
+            )
+        )
+    ]
+    for load in loads:
+        load.start()
 
     def flow_copy(k):
         partner = lax.rem(me + k, groups)
@@ -162,12 +190,23 @@
             device_id_type=mesh_ids,
         )
 
+    for load in loads[:6]:
+        load.wait()
     for at, current in ((0, u_ref), (1, v_ref)):
         flow = jnp.dot(
             weight_ref[...], current[...], precision=highest, preferred_element_type=jnp.float32
         )
         for c in range(cores):
             flow_send[c, at * freqs : (at + 1) * freqs, :] = flow[c * freqs : (c + 1) * freqs]
+
+    for at, rate, factor in ((0, wind_ref, gain_ref), (1, dissipation_ref, damping_ref)):
+        factor[...] = lax.dot_general(
+            spread_ref[at],
+            jnp.broadcast_to(rate[...], (columns, freq_count)),
+            (((1,), (1,)), ((), ())),
+            precision=highest,
+            preferred_element_type=jnp.float32,
+        )
 
     planes_beside = jnp.minimum(plane, 1) + jnp.minimum(planes - 1 - plane, 1)
     pl.semaphore_wait(barrier, groups - 1 + groups * planes_beside)
@@ -194,7 +233,7 @@
         )
         energy = jnp.sum(spectra * spectra, axis=0, keepdims=True) * (1.0 / spectra.shape[0])
         held[...] = (
-            sea_own_ref[...]
+            sea_ref[pl.ds(me, 1), :].astype(jnp.float32)
             * (spectra * (1.0 + time_step * gain_ref[...]) + time_step * redist)
             / (1.0 + time_step * damping_ref[...] * energy)
         )
@@ -232,7 +271,7 @@
                     edge_copy(stage, side, level, r, r).wait_recv()
                 order[...] = jnp.zeros_like(order)
                 for y in range(rows):
-                    order[y : y + 1, :] = edge_recv[stage][side][wanted[y], side : side + 1, :]
+                    order[y : y + 1, :] = edge_recv[stage][side][wanted[0, y], side : side + 1, :]
                 square = (padded, padded)
                 unit = lax.broadcasted_iota(jnp.int32, square, 0) == lax.broadcasted_iota(
                     jnp.int32, square, 1
@@ -343,7 +382,8 @@
                     f * dirs : (f + 1) * dirs
                 ]
 
-    loads[0].wait()
+    for load in loads[6:-1]:
+        load.wait()
     sources(0, spectrum_ref[...])
     for k in range(1, groups):
         source = lax.rem(me + groups - k, groups)
@@ -371,7 +411,7 @@
     for g, d, here in natural:
         held[here : here + freqs, :] = recv[1, g, pl.ds(d, freqs, stride=dirs), :]
     sources(1, held[...])
-    loads[1].wait()
+    loads[-1].wait()
     stokes_ref[...] = jnp.dot(
         drift_ref[...], held[...], precision=highest, preferred_element_type=jnp.float32
     )
@@ -422,9 +462,6 @@
     chunks = 3 if padded % (3 * tile) == 0 else 1
     width = rounded_up(padded, 128)
     flow_rows = rounded_up(2 * freq_local, 8)
-    space_rank = lax.axis_index("space")
-    core_rank = lax.axis_index("spec")
-    block_rank = space_rank * cores + core_rank
     angles, current_weight, drifts = tables(freq_count, directions, levels)
     cosines, sines = np.cos(angles), np.sin(angles)
     cosines[np.abs(cosines) < 1e-12] = 0.0
@@ -434,17 +471,14 @@
     courant = courant.reshape(2, ranks, dir_local, cores, freq_local).transpose(1, 3, 0, 4, 2)
     courant = courant.reshape(groups, 2, comps_local, 1).astype(np.float32)
     courant = np.pad(courant, ((0, 0), (0, 0), (0, padded - comps_local), (0, 0)))
-    courant = lax.dynamic_index_in_dim(jnp.asarray(courant), block_rank, 0, keepdims=False)
 
     trig = np.stack([cosines, sines]) * stokes_gain / math.sqrt(directions)
     stokes_table = trig[:, None, :, None] * drifts.T[None, :, None, :]
     stokes_table = stokes_table.reshape(2 * levels, components).astype(np.float32)
 
-    heading = jnp.asarray((0.5 * (1.0 + cosines)).astype(np.float32))
-    gain = (heading[:, None] * wind_rate[None, :]).reshape(components, 1)
-    damping = jnp.broadcast_to(dissipation[None, :], (directions, freq_count))
-    damping = damping.reshape(components, 1)
-    sea_own = lax.dynamic_slice_in_dim(land_sea[0], block_rank, 1, 0).astype(jnp.float32)
+    heading = np.repeat(0.5 * (1.0 + cosines), freq_count)[:, None]
+    unit = np.tile(np.eye(freq_count), (directions, 1))
+    spread = np.stack([heading * unit, unit]).astype(np.float32)
     f32 = jnp.float32
     waves, stokes = pl.pallas_call(
         functools.partial(
@@ -454,11 +488,24 @@
             jax.ShapeDtypeStruct((comps_local * total_rows, columns), f32),
             jax.ShapeDtypeStruct((2 * levels, columns), f32),
         ),
-        in_specs=[vmem] * 3 + [smem] * 2 + [vmem] * 6 + [anywhere] * 2,
+        in_specs=[in_place] * 13,
         out_specs=(vmem, vmem),
         scratch_shapes=[
+            pltpu.VMEM((levels, columns), f32),
+            pltpu.VMEM((levels, columns), f32),
+            pltpu.VMEM(current_weight.shape, f32),
+            pltpu.VMEM((1, freq_count), f32),
+            pltpu.VMEM((1, freq_count), f32),
+            pltpu.VMEM(spread.shape, f32),
+            pltpu.VMEM((components, columns), f32),
             pltpu.VMEM(transfer.shape, transfer.dtype),
+            pltpu.VMEM(land_sea.shape[1:], land_sea.dtype),
+            pltpu.VMEM(courant.shape[1:], f32),
+            pltpu.SMEM(west_index.shape, west_index.dtype),
+            pltpu.SMEM(east_index.shape, east_index.dtype),
             pltpu.VMEM(stokes_table.shape, f32),
+            pltpu.VMEM((components, columns), f32),
+            pltpu.VMEM((components, columns), f32),
             pltpu.VMEM((components, columns), f32),
             pltpu.VMEM((cores, flow_rows, columns), f32),
             pltpu.VMEM((groups, flow_rows, columns), f32),
@@ -473,7 +520,7 @@
             pltpu.VMEM((groups, 8, width), f32),
             pltpu.VMEM((columns, width), f32),
             pltpu.VMEM((2, padded, columns), f32),
-            pltpu.SemaphoreType.DMA((2,)),
+            pltpu.SemaphoreType.DMA((13,)),
             pltpu.SemaphoreType.DMA((3, chunks, groups)),
             pltpu.SemaphoreType.DMA((3, chunks, groups)),
             pltpu.SemaphoreType.DMA((groups,)),
@@ -482,22 +529,22 @@
             pltpu.SemaphoreType.DMA((2, 2, groups)),
         ],
         compiler_params=pltpu.CompilerParams(
-            collective_id=0, has_side_effects=True, vmem_limit_bytes=48 * 1024 * 1024
+            collective_id=0, has_side_effects=True, vmem_limit_bytes=40 * 1024 * 1024
         ),
         name="waves",
     )(
-        spectrum[0].reshape(components, columns),
-        sea_own,
-        land_sea[0],
-        west_index[0],
-        east_index[0],
         current_u[0].reshape(levels, columns),
         current_v[0].reshape(levels, columns),
         jnp.asarray(current_weight),
-        gain,
-        damping,
-        courant,
+        wind_rate.reshape(1, freq_count),
+        dissipation.reshape(1, freq_count),
+        jnp.asarray(spread),
+        spectrum[0].reshape(components, columns),
         transfer,
+        land_sea[0],
+        jnp.asarray(courant),
+        west_index,
+        east_index,
         jnp.asarray(stokes_table),
     )
     return (

time: 51 us -> 50.6 us (level)
  local copies, waits for them, and re-layouts: 11.5 us -> 13.4 us
  other arithmetic: 1.44 us -> 0 us
  Pallas kernels: 36.7 us -> 35.8 us
    unnamed x20 -> x28, local copies, waits for them, and re-layouts: 9.56 us -> 13.4 us
    pallas_call x1, Pallas kernels: 36.7 us -> 35.8 us  [shards(): pl.pallas_call(functools.partial(wave_kernel, ranks, cores, dir_local, fr...]
    squeeze x2 -> x0, local copies, waits for them, and re-layouts: 0.82 us -> none  [shards(): lax.dynamic_index_in_dim(jnp.asarray(courant), block_rank, 0, keepdims=Fa...]
    mul x1 -> x0, other arithmetic: 0.74 us -> none  [shards(): gain = (heading[:, None] * wind_rate[None, :]).reshape(components, 1)]
    convert_element_type x1 -> x0, other arithmetic: 0.7 us -> none  [shards(): lax.dynamic_slice_in_dim(land_sea[0], block_rank, 1, 0).astype(jnp.float32)]
    broadcast_in_dim x1 -> x0, local copies, waits for them, and re-layouts: 0.66 us -> none  [shards(): damping = jnp.broadcast_to(dissipation[None, :], (directions, freq_count))]
where the time goes in v2:
time: 50.6 us; the launch traced here: 49.8 us
  Pallas kernels  35.8 us (71%)
  local copies, waits for them, and re-layouts  13.4 us (26%)
  between operations  0.66 us (1%)
    pallas_call x1, Pallas kernels, shards(): pl.pallas_call(functools.partial(wave_kernel, ranks, cores, dir_local, fr...  35.8 us
    unnamed x28, local copies, waits for them, and re-layouts  13.4 us

profile of v2, /device:TPU:0, one launch (start us, length us, event | category | flops | bytes accessed | tf_op | source)
XLA Modules:
  0.0 49.8 jit_solution(8867395092223181644)
XLA Ops:
  0.6 0.0 copy-start
  0.6 1.7 %copy-done = bf16[1152,1152]{1,0:T(8,128)(2,1)S(1)} copy-done((bf16[1152,1152]{1,0:T(8,128)(2,1)S(1)}, bf16[1152,1152]{1,0:T(8,128)(2,1)}, u32[]{:S(2)}) %copy-start) | copy-done | bytes 2654232
  2.4 0.0 copy-start.1
  2.4 1.3 %copy-done.1 = f32[8,2,144,1]{3,2,1,0:T(8,128)S(1)} copy-done((f32[8,2,144,1]{3,2,1,0:T(8,128)S(1)}, f32[8,2,144,1]{3,2,1,0:T(8,128)}, u32[]{:S(2)}) %copy-start.1) | copy-done | bytes 9240
  3.7 0.0 copy-start.2
  3.7 1.3 %copy-done.2 = f32[2,1152,36]{2,1,0:T(8,128)S(1)} copy-done((f32[2,1152,36]{2,1,0:T(8,128)S(1)}, f32[2,1152,36]{2,1,0:T(8,128)}, u32[]{:S(2)}) %copy-start.2) | copy-done | bytes 331800
  4.9 0.0 copy-start.3
  4.9 1.1 %copy-done.3 = f32[1,32,36,1,128]{4,3,2,1,0:T(1,128)S(1)} copy-done((f32[1,32,36,1,128]{4,3,2,1,0:T(1,128)S(1)}, f32[1,32,36,1,128]{4,3,2,1,0:T(1,128)}, u32[]{:S(2)}) %copy-start.3) | copy-done | bytes 589848
  6.0 0.0 copy-start.4
  6.0 1.1 %copy-done.4 = f32[128,1152]{1,0:T(8,128)S(1)} copy-done((f32[128,1152]{1,0:T(8,128)S(1)}, f32[128,1152]{1,0:T(8,128)}, u32[]{:S(2)}) %copy-start.4) | copy-done | bytes 589848
  7.1 0.0 copy-start.5
  7.1 0.8 %copy-done.5 = f32[1,64,1,128]{3,2,1,0:T(1,128)S(1)} copy-done((f32[1,64,1,128]{3,2,1,0:T(1,128)S(1)}, f32[1,64,1,128]{3,2,1,0:T(1,128)}, u32[]{:S(2)}) %copy-start.5) | copy-done | bytes 32792
  7.8 0.0 copy-start.6
  7.8 0.8 %copy-done.6 = f32[1,64,1,128]{3,2,1,0:T(1,128)S(1)} copy-done((f32[1,64,1,128]{3,2,1,0:T(1,128)S(1)}, f32[1,64,1,128]{3,2,1,0:T(1,128)}, u32[]{:S(2)}) %copy-start.6) | copy-done | bytes 32792
  8.6 0.0 copy-start.7
  8.6 0.7 %copy-done.7 = f32[36,64]{1,0:T(8,128)S(1)} copy-done((f32[36,64]{1,0:T(8,128)S(1)}, f32[36,64]{1,0:T(8,128)}, u32[]{:S(2)}) %copy-start.7) | copy-done | bytes 9240
  9.3 0.0 copy-start.8
  9.3 0.7 %copy-done.8 = s32[1,8,128]{2,1,0:T(8,128)S(1)} copy-done((s32[1,8,128]{2,1,0:T(8,128)S(1)}, s32[1,8,128]{2,1,0:T(8,128)}, u32[]{:S(2)}) %copy-start.8) | copy-done | bytes 4120
  10.0 0.0 copy-start.9
  10.0 0.7 %copy-done.9 = f32[36]{0:T(128)S(1)} copy-done((f32[36]{0:T(128)S(1)}, f32[36]{0:T(128)}, u32[]{:S(2)}) %copy-start.9) | copy-done | bytes 168
  10.6 0.0 copy-start.10
  10.6 0.7 %copy-done.10 = f32[36]{0:T(128)S(1)} copy-done((f32[36]{0:T(128)S(1)}, f32[36]{0:T(128)}, u32[]{:S(2)}) %copy-start.10) | copy-done | bytes 168
  11.3 0.0 copy-start.11
  11.3 0.7 %copy-done.11 = s32[1,8]{1,0:T(1,128)S(1)} copy-done((s32[1,8]{1,0:T(1,128)S(1)}, s32[1,8]{1,0:T(1,128)}, u32[]{:S(2)}) %copy-start.11) | copy-done | bytes 56
  12.0 0.0 copy-start.12
  12.0 0.7 %copy-done.12 = s32[1,8]{1,0:T(1,128)S(1)} copy-done((s32[1,8]{1,0:T(1,128)S(1)}, s32[1,8]{1,0:T(1,128)}, u32[]{:S(2)}) %copy-start.12) | copy-done | bytes 56
  12.6 35.8 %waves.1 = (f32[1152,128]{1,0:T(8,128)S(1)}, f32[128,128]{1,0:T(8,128)S(1)}) custom-call(f32[64,128]{1,0:T(8,128)S(1)} %bitcast.13, f32[64,128]{1,0:T(8,128)S(1)} %bitcast.14, f32[36,64]{1,0:T(8,128)S(1)} %copy-done.7, f32[1,36]{1,0:T(1,128)S(1)} %bitcast.16, f32[1,36]{1,0:T(1,128)S(1)} %bitcast.17, f32[2,1152,36]{2,1,0:T(8,128)S(1)} %copy-done.2, ...), custom_call_target="tpu_custom_call" | custom-call | tf_op jit(solution)/shard_map/waves/pallas_call | solution.py:483
  48.4 0.8 %copy.18 = f32[1,8,18,8,128]{4,3,2,1,0:T(8,128)} copy(f32[1,8,18,8,128]{4,3,2,1,0:T(8,128)S(1)} %bitcast.11) | data formatting | bytes 1179648
  49.2 0.6 %copy.19 = f32[1,128,1,128]{3,2,1,0:T(1,128)} copy(f32[1,128,1,128]{3,2,1,0:T(1,128)S(1)} %bitcast.12) | data formatting | bytes 131072
Async XLA Ops:
  0.6 1.8 %copy-start = (bf16[1152,1152]{1,0:T(8,128)(2,1)S(1)}, bf16[1152,1152]{1,0:T(8,128)(2,1)}, u32[]{:S(2)}) copy-start(bf16[1152,1152]{1,0:T(8,128)(2,1)} %transfer_hbm.1) | copy-start | bytes 7962628
  2.4 1.3 %copy-start.1 = (f32[8,2,144,1]{3,2,1,0:T(8,128)S(1)}, f32[8,2,144,1]{3,2,1,0:T(8,128)}, u32[]{:S(2)}) copy-start(f32[8,2,144,1]{3,2,1,0:T(8,128)} %constant.10.clone.courant_hbm) | copy-start | bytes 27652
  3.7 1.3 %copy-start.2 = (f32[2,1152,36]{2,1,0:T(8,128)S(1)}, f32[2,1152,36]{2,1,0:T(8,128)}, u32[]{:S(2)}) copy-start(f32[2,1152,36]{2,1,0:T(8,128)} %constant.9.clone.spread_hbm) | copy-start | bytes 995332
  4.9 1.1 %copy-start.3 = (f32[1,32,36,1,128]{4,3,2,1,0:T(1,128)S(1)}, f32[1,32,36,1,128]{4,3,2,1,0:T(1,128)}, u32[]{:S(2)}) copy-start(f32[1,32,36,1,128]{4,3,2,1,0:T(1,128)} %param.13) | copy-start | bytes 1769476
  6.0 1.1 %copy-start.4 = (f32[128,1152]{1,0:T(8,128)S(1)}, f32[128,1152]{1,0:T(8,128)}, u32[]{:S(2)}) copy-start(f32[128,1152]{1,0:T(8,128)} %constant.11.clone.drift_hbm) | copy-start | bytes 1769476
  7.1 0.8 %copy-start.5 = (f32[1,64,1,128]{3,2,1,0:T(1,128)S(1)}, f32[1,64,1,128]{3,2,1,0:T(1,128)}, u32[]{:S(2)}) copy-start(f32[1,64,1,128]{3,2,1,0:T(1,128)} %param.17) | copy-start | bytes 98308
  7.8 0.8 %copy-start.6 = (f32[1,64,1,128]{3,2,1,0:T(1,128)S(1)}, f32[1,64,1,128]{3,2,1,0:T(1,128)}, u32[]{:S(2)}) copy-start(f32[1,64,1,128]{3,2,1,0:T(1,128)} %param.18) | copy-start | bytes 98308
  8.6 0.7 %copy-start.7 = (f32[36,64]{1,0:T(8,128)S(1)}, f32[36,64]{1,0:T(8,128)}, u32[]{:S(2)}) copy-start(f32[36,64]{1,0:T(8,128)} %constant.8.clone.weight_hbm) | copy-start | bytes 27652
  9.3 0.7 %copy-start.8 = (s32[1,8,128]{2,1,0:T(8,128)S(1)}, s32[1,8,128]{2,1,0:T(8,128)}, u32[]{:S(2)}) copy-start(s32[1,8,128]{2,1,0:T(8,128)} %param.14) | copy-start | bytes 12292
  10.0 0.7 %copy-start.9 = (f32[36]{0:T(128)S(1)}, f32[36]{0:T(128)}, u32[]{:S(2)}) copy-start(f32[36]{0:T(128)} %param.20) | copy-start | bytes 436
  10.6 0.7 %copy-start.10 = (f32[36]{0:T(128)S(1)}, f32[36]{0:T(128)}, u32[]{:S(2)}) copy-start(f32[36]{0:T(128)} %param.21) | copy-start | bytes 436
  11.3 0.7 %copy-start.11 = (s32[1,8]{1,0:T(1,128)S(1)}, s32[1,8]{1,0:T(1,128)}, u32[]{:S(2)}) copy-start(s32[1,8]{1,0:T(1,128)} %west_hbm.1) | copy-start | bytes 100
  12.0 0.7 %copy-start.12 = (s32[1,8]{1,0:T(1,128)S(1)}, s32[1,8]{1,0:T(1,128)}, u32[]{:S(2)}) copy-start(s32[1,8]{1,0:T(1,128)} %east_hbm.1) | copy-start | bytes 100

commit v3 on v2

--- a/solution.py
+++ b/solution.py
@@ -17,7 +17,6 @@
 stokes_gain = 2.0
 highest = lax.Precision.HIGHEST
 mesh_ids = pl.DeviceIdType.MESH
-vmem = pl.BlockSpec(memory_space=pltpu.VMEM)
 in_place = pl.BlockSpec(memory_space=pltpu.HBM)
 
 
@@ -54,6 +53,8 @@
     west_hbm,
     east_hbm,
     drift_hbm,
+    waves_hbm,
+    stokes_hbm,
     waves_ref,
     stokes_ref,
     u_ref,
@@ -86,6 +87,8 @@
     order,
     ghosts,
     load_sem,
+    waves_sem,
+    stokes_sem,
     send_sem,
     recv_sem,
     flow_send_sem,
@@ -190,6 +193,17 @@
             device_id_type=mesh_ids,
         )
 
+    def store_waves(ch, d):
+        lines = min(piece // dirs, freqs) * rows
+        part = pl.ds(pl.multiple_of(d * freqs * rows + ch * lines, 8), lines)
+        return pltpu.make_async_copy(
+            waves_ref.at[part], waves_hbm.at[part], waves_sem.at[ch, d]
+        )
+
+    def give_waves(ch):
+        for d in range(dirs):
+            store_waves(ch, d).start()
+
     for load in loads[:6]:
         load.wait()
     for at, current in ((0, u_ref), (1, v_ref)):
@@ -415,9 +429,15 @@
     stokes_ref[...] = jnp.dot(
         drift_ref[...], held[...], precision=highest, preferred_element_type=jnp.float32
     )
+    stokes_store = pltpu.make_async_copy(stokes_ref, stokes_hbm, stokes_sem)
+    stokes_store.start()
     border(1)
-    propagate(2, emit_waves, lambda ch: None)
-
+    propagate(2, emit_waves, give_waves)
+
+    for ch in range(chunks):
+        for d in range(dirs):
+            store_waves(ch, d).wait()
+    stokes_store.wait()
     for k in range(1, groups):
         flow_copy(k).wait_send()
         for phase in range(3):
@@ -489,8 +509,10 @@
             jax.ShapeDtypeStruct((2 * levels, columns), f32),
         ),
         in_specs=[in_place] * 13,
-        out_specs=(vmem, vmem),
+        out_specs=(in_place, in_place),
         scratch_shapes=[
+            pltpu.VMEM((comps_local * total_rows, columns), f32),
+            pltpu.VMEM((2 * levels, columns), f32),
             pltpu.VMEM((levels, columns), f32),
             pltpu.VMEM((levels, columns), f32),
             pltpu.VMEM(current_weight.shape, f32),
@@ -521,6 +543,8 @@
             pltpu.VMEM((columns, width), f32),
             pltpu.VMEM((2, padded, columns), f32),
             pltpu.SemaphoreType.DMA((13,)),
+            pltpu.SemaphoreType.DMA((chunks, dir_local)),
+            pltpu.SemaphoreType.DMA(()),
             pltpu.SemaphoreType.DMA((3, chunks, groups)),
             pltpu.SemaphoreType.DMA((3, chunks, groups)),
             pltpu.SemaphoreType.DMA((groups,)),
@@ -529,7 +553,7 @@
             pltpu.SemaphoreType.DMA((2, 2, groups)),
         ],
         compiler_params=pltpu.CompilerParams(
-            collective_id=0, has_side_effects=True, vmem_limit_bytes=40 * 1024 * 1024
+            collective_id=0, has_side_effects=True, vmem_limit_bytes=64 * 1024 * 1024
         ),
         name="waves",
     )(

time: 50.6 us -> 40.4 us (0.80)
  local copies, waits for them, and re-layouts: 13.4 us -> 2.58 us
  Pallas kernels: 35.8 us -> 36.9 us
    unnamed x28 -> x4, local copies, waits for them, and re-layouts: 13.4 us -> 2.58 us
    pallas_call x1, Pallas kernels: 35.8 us -> 36.9 us  [shards(): pl.pallas_call(functools.partial(wave_kernel, ranks, cores, dir_local, fr...]
where the time goes in v3:
time: 40.4 us; the launch traced here: 40.1 us
  Pallas kernels  36.9 us (91%)
  local copies, waits for them, and re-layouts  2.58 us (6%)
  between operations  0.65 us (2%)
    pallas_call x1, Pallas kernels, shards(): pl.pallas_call(functools.partial(wave_kernel, ranks, cores, dir_local, fr...  36.9 us
    unnamed x4, local copies, waits for them, and re-layouts  2.58 us

profile of v3, /device:TPU:0, one launch (start us, length us, event | category | flops | bytes accessed | tf_op | source)
XLA Modules:
  0.0 40.1 jit_solution(11627747124528042729)
XLA Ops:
  0.6 36.9 %waves.1 = (f32[1152,128]{1,0:T(8,128)}, f32[128,128]{1,0:T(8,128)}) custom-call(f32[64,128]{1,0:T(8,128)} %bitcast.13, f32[64,128]{1,0:T(8,128)} %bitcast.14, f32[36,64]{1,0:T(8,128)} %constant.8.clone.weight_hbm, f32[1,36]{1,0:T(1,128)} %bitcast.16, f32[1,36]{1,0:T(1,128)} %bitcast.17, f32[2,1152,36]{2,1,0:T(8,128)} %constant.9.clone.spread_hbm, ...), custom_call_target="tpu_custom_call" | custom-call | tf_op jit(solution)/shard_map/waves/pallas_call | solution.py:503
  37.5 0.0 copy-start
  37.5 1.9 %copy.18 = f32[1,8,18,8,128]{4,3,2,1,0:T(8,128)} copy(f32[1,8,18,8,128]{4,3,2,1,0:T(8,128)} %bitcast.11) | data formatting | bytes 1179648
  39.5 0.0 copy-done
  39.5 0.6 %copy.19 = f32[1,128,1,128]{3,2,1,0:T(1,128)} copy(f32[1,128,1,128]{3,2,1,0:T(1,128)S(1)} %bitcast.12) | data formatting | bytes 131072
Async XLA Ops:
  37.5 2.0 %copy-start = (f32[128,128]{1,0:T(8,128)S(1)}, f32[128,128]{1,0:T(8,128)}, u32[]{:S(2)}) copy-start(f32[128,128]{1,0:T(8,128)} %get-tuple-element.5) | copy-start | bytes 196612

commit v4 on v3

--- a/solution.py
+++ b/solution.py
@@ -364,7 +364,7 @@
             lines[y] = lines[y] + down * lines[y - 1]
         for y in range(rows - 2, -1, -1):
             lines[y] = lines[y] + up * lines[y + 1]
-        return [sea_ref[y : y + 1, :].astype(jnp.float32) * lines[y] for y in range(rows)]
+        return lines
 
     def propagate(phase, emit, after):
         def chunk(ch, carry):
@@ -380,7 +380,8 @@
 
     def emit_send(base, lines):
         for y in range(rows):
-            send[1, y, pl.ds(pl.multiple_of(base, 8), tile), :] = lines[y]
+            sea = sea_ref[y : y + 1, :].astype(jnp.float32)
+            send[1, y, pl.ds(pl.multiple_of(base, 8), tile), :] = sea * lines[y]
 
     def send_piece(ch):
         for k in range(1, groups):
@@ -479,7 +480,7 @@
     groups = ranks * cores
     padded = rounded_up(comps_local, 8)
     tile = 24 if padded % 24 == 0 else 8
-    chunks = 3 if padded % (3 * tile) == 0 else 1
+    chunks = 6 if padded % (6 * tile) == 0 else 1
     width = rounded_up(padded, 128)
     flow_rows = rounded_up(2 * freq_local, 8)
     angles, current_weight, drifts = tables(freq_count, directions, levels)
@@ -492,7 +493,7 @@
     courant = courant.reshape(groups, 2, comps_local, 1).astype(np.float32)
     courant = np.pad(courant, ((0, 0), (0, 0), (0, padded - comps_local), (0, 0)))
 
-    trig = np.stack([cosines, sines]) * stokes_gain / math.sqrt(directions)
+    trig = np.stack([cosines, sines])
     stokes_table = trig[:, None, :, None] * drifts.T[None, :, None, :]
     stokes_table = stokes_table.reshape(2 * levels, components).astype(np.float32)
 
@@ -571,9 +572,11 @@
         east_index,
         jnp.asarray(stokes_table),
     )
+    waves = waves.reshape(1, dir_local, freq_local, total_rows, columns)
+    stokes = stokes.reshape(1, 2 * levels, rows_local, columns)
     return (
-        waves.reshape(1, dir_local, freq_local, total_rows, columns),
-        stokes.reshape(1, 2 * levels, rows_local, columns),
+        waves * land_sea[0].astype(f32),
+        stokes * np.float32(stokes_gain / math.sqrt(directions)),
     )
 
 

time: 40.4 us -> 44.4 us (1.099)
  other arithmetic: 0 us -> 3.87 us
  Pallas kernels: 36.9 us -> 39.7 us
  local copies, waits for them, and re-layouts: 2.58 us -> 0.01 us
    pallas_call x1, Pallas kernels: 36.9 us -> 39.7 us  [shards(): pl.pallas_call(functools.partial(wave_kernel, ranks, cores, dir_local, fr...]
    mul x0 -> x2, other arithmetic: none -> 2.59 us  [the longest x1 1.95 us: shards(): waves * land_sea[0].astype(f32)]
    unnamed x4 -> x2, local copies, waits for them, and re-layouts: 2.58 us -> 0.01 us
    convert_element_type x0 -> x1, other arithmetic: none -> 1.28 us  [shards(): land_sea[0].astype(f32)]
where the time goes in v4:
time: 44.4 us; the launch traced here: 44.2 us
  Pallas kernels  39.7 us (89%)
  other arithmetic  3.87 us (9%)
  between operations  0.65 us (1%)
    pallas_call x1, Pallas kernels, shards(): pl.pallas_call(functools.partial(wave_kernel, ranks, cores, dir_local, fr...  39.7 us
    mul x1, other arithmetic, shards(): waves * land_sea[0].astype(f32)  1.95 us
    convert_element_type x1, other arithmetic, shards(): land_sea[0].astype(f32)  1.28 us

profile of v4, /device:TPU:0, one launch (start us, length us, event | category | flops | bytes accessed | tf_op | source)
XLA Modules:
  0.0 44.2 jit_solution(15166537077122340485)
XLA Ops:
  0.6 1.3 %bitcast_convert_fusion = f32[8,128]{1,0:T(8,128)} fusion(s32[1,8,128]{2,1,0:T(8,128)} %param.14), kind=kLoop, calls=%fused_computation.2 | loop fusion | flops 1024 | bytes 8192 | tf_op jit(solution)/shard_map/convert_element_type | solution.py:578
  1.9 39.7 %waves.1 = (f32[1152,128]{1,0:T(8,128)}, f32[128,128]{1,0:T(8,128)}) custom-call(f32[64,128]{1,0:T(8,128)} %bitcast.14, f32[64,128]{1,0:T(8,128)} %bitcast.15, f32[36,64]{1,0:T(8,128)} %constant.10.clone.weight_hbm, f32[1,36]{1,0:T(1,128)} %bitcast.17, f32[1,36]{1,0:T(1,128)} %bitcast.18, f32[2,1152,36]{2,1,0:T(8,128)} %constant.11.clone.spread_hbm, ...), custom_call_target="tpu_custom_call" | custom-call | tf_op jit(solution)/shard_map/waves/pallas_call | solution.py:504
  41.6 0.0 copy-start
  41.6 2.0 %broadcast_multiply_fusion = f32[1,8,18,8,128]{4,3,2,1,0:T(8,128)} fusion(f32[1,8,18,8,128]{4,3,2,1,0:T(8,128)} %bitcast.12, f32[8,128]{1,0:T(8,128)} %bitcast_convert_fusion), kind=kLoop, calls=%fused_computation | loop fusion | flops 147456 | bytes 1183744 | tf_op jit(solution)/shard_map/mul | solution.py:578
  43.6 0.0 copy-done
  43.6 0.6 %broadcast_multiply_fusion.1 = f32[128,128]{1,0:T(8,128)} fusion(f32[128,128]{1,0:T(8,128)S(1)} %copy-done), kind=kLoop, calls=%fused_computation.1 | loop fusion | flops 16384 | bytes 131072 | tf_op jit(solution)/shard_map/mul | solution.py:579
Async XLA Ops:
  41.6 2.0 %copy-start = (f32[128,128]{1,0:T(8,128)S(1)}, f32[128,128]{1,0:T(8,128)}, u32[]{:S(2)}) copy-start(f32[128,128]{1,0:T(8,128)} %get-tuple-element.5) | copy-start | bytes 196612
